TPU v7x, 32 devices: a whole 2x2x4 slice. The times are simulated.
32 devices in a mesh: row: 4 (over y, x), col: 8 (over z, core).
Axes of the slice: x: 2, y: 2, z: 4, core: 2. Of those that a mesh axis runs over, the one named last changes fastest.
Arguments:
- panel_left: bfloat16 [5000, 32, 128], P(None, ('row', 'col')), may hold values from -0.078125 to 0.078125
- panel_right: bfloat16 [5000, 32, 128], P(None, ('row', 'col')), may hold values from -6 to 6
- amplitudes: bfloat16 [128, 128, 128], P('col', 'row'), may hold values from -0.046875 to 0.046875
- eps_virtual: float32 [1600], replicated, may hold values from 0.2 to 1.5
- eps_occupied: float32 [100], replicated, may hold values from -1.5 to -0.3
- pair_list: int32 [128, 2], replicated, may hold values from 0 to 99
- blocks: int32 [2], replicated, may hold values from 0 to 49
Outputs:
- update: bfloat16 [128, 32, 32], P('col', 'row')
All inputs are finite; a program needn't handle non-finite values.
Results may differ from a plain program's by a relative error of at most 0.0049.
Values may be sent and summed in bfloat16 or wider, within the bound.
A program may use at most 128 MiB of HBM per device.

v0:
```python
import functools

import jax
import jax.numpy as jnp
from jax import lax
from jax.experimental import pallas as pl
from jax.experimental.pallas import tpu as pltpu
from jax.sharding import PartitionSpec as P

MESH = pl.DeviceIdType.MESH
F32 = jnp.float32
BF16 = jnp.bfloat16


def arrival(ref, sem):
    pltpu.make_async_copy(ref, ref, sem).wait()


def kernel(
    row_n, col_n, base, extra,
    left, right, tails, amps, eps_v, eps_o, pairs, blocks,
    out,
    lbuf, rbuf, lturn, lrows, tbuf, tturn, ybuf, acc, out1, in1, fin, out2, in2, den,
    l_send, l_recv, r_send, r_recv, t_send1, t_send2, t_send3, t_recv,
    s1_send, s1_recv, s2_send, s2_recv,
):
    n = row_n * col_n
    pairs_of_cols = col_n // 2
    slots = 2 * row_n
    cb, pb, width = amps.shape
    all_c = cb * row_n
    all_p = pb * col_n
    kp = lbuf.shape[1]
    few, most = 16 * base, 16 * (base + 1)
    a_own = n // row_n
    row = lax.axis_index("row")
    col = lax.axis_index("col")
    me = row * col_n + col
    cpair = col // 2
    half = col % 2

    barrier = pltpu.get_barrier_semaphore()

    def greet(e, _):
        d = (me + e) % n
        pl.semaphore_signal(barrier, inc=1, device_id=(d // col_n, d % col_n), device_id_type=MESH)
        return 0

    lax.fori_loop(1, n, greet, 0)

    def t_block(r, c):
        return tbuf.at[pl.ds(r * cb, cb), pl.ds(c * pb, pb), :]

    pltpu.make_async_copy(amps, t_block(row, col), t_recv.at[me]).start()

    def shares(src, which, dst, d, copy, act):
        @pl.when(d < extra)
        def _():
            act(copy(src.at[pl.ds(d * most, most), :], dst.at[pl.ds(0, most), :]))

        @pl.when((d >= extra) & (d < n - 1))
        def _():
            at = extra * most + (d - extra) * few
            act(copy(src.at[pl.ds(at, few), :], dst.at[pl.ds(0, few), :]))

        @pl.when(d == n - 1)
        def _():
            at = extra * most + (n - 1 - extra) * few
            act(copy(src.at[pl.ds(at, few - 16), :], dst.at[pl.ds(0, few - 16), :]))
            act(copy(tails.at[which], dst.at[pl.ds(few - 16, 16), :]))

    def share_arrival(ref, sem):
        @pl.when(me < extra)
        def _():
            arrival(ref.at[pl.ds(0, most), :], sem)

        @pl.when(me >= extra)
        def _():
            arrival(ref.at[pl.ds(0, few), :], sem)

    def begin(copy):
        copy.start()

    def begun(copy):
        copy.wait_send()

    shares(left, 0, lbuf.at[me], me, lambda a, b: pltpu.make_async_copy(a, b, l_recv.at[me]), begin)
    shares(
        right, 1, rbuf.at[0, row * 2 + half], me,
        lambda a, b: pltpu.make_async_copy(a, b, r_recv.at[me]), begin,
    )

    def clear(at):
        def one(i, _):
            lbuf[i, pl.ds(at, kp - at), :] = jnp.zeros((kp - at, width), BF16)
            rbuf[i // slots, i % slots, pl.ds(at, kp - at), :] = jnp.zeros((kp - at, width), BF16)
            return 0

        lax.fori_loop(0, n, one, 0)

    if kp > most:
        @pl.when(me < extra)
        def _():
            clear(most)

    @pl.when(me >= extra)
    def _():
        clear(few)

    pl.semaphore_wait(barrier, n - 1)

    def mate(i):
        return 2 * ((cpair + i) % pairs_of_cols) + half

    def t1_copy(s, up):
        c = 2 * (cpair - s if up else cpair + s) + half
        to = 2 * (cpair + 1 if up else cpair - 1) + half
        return pltpu.make_async_remote_copy(
            src_ref=t_block(row, c), dst_ref=t_block(row, c),
            send_sem=t_send1.at[2 * s + (1 if up else 0)], recv_sem=t_recv.at[row * col_n + c],
            device_id=(row, to), device_id_type=MESH,
        )

    def t1_when(s, up):
        if up:
            return (cpair >= s) & (cpair < pairs_of_cols - 1)
        return (cpair + s < pairs_of_cols) & (cpair > 0)

    def t1_step(s):
        for up in (False, True):
            if s > 0:
                @pl.when(cpair >= s if up else cpair + s < pairs_of_cols)
                def _():
                    at = row * col_n + 2 * (cpair - s if up else cpair + s) + half
                    c = 2 * (cpair - s if up else cpair + s) + half
                    arrival(t_block(row, c), t_recv.at[at])

            @pl.when(t1_when(s, up))
            def _():
                t1_copy(s, up).start()

    def t2_copy(i, e):
        c = mate(i)
        return pltpu.make_async_remote_copy(
            src_ref=t_block(row, c), dst_ref=t_block(row, c),
            send_sem=t_send2.at[i * row_n + e], recv_sem=t_recv.at[row * col_n + c],
            device_id=((row + e) % row_n, col), device_id_type=MESH,
        )

    def t3_copy(i, e):
        c, r = mate(i), (row + e) % row_n
        return pltpu.make_async_remote_copy(
            src_ref=t_block(r, c), dst_ref=t_block(r, c),
            send_sem=t_send3.at[i * row_n + e], recv_sem=t_recv.at[r * col_n + c],
            device_id=(row, 2 * cpair + 1 - half), device_id_type=MESH,
        )

    def target(k, j):
        spot = (row * 2 + half + j) % slots
        return (spot // 2) * col_n + 2 * ((cpair + pairs_of_cols - k) % pairs_of_cols) + spot % 2

    def remote(send, recv, d):
        return lambda a, b: pltpu.make_async_remote_copy(
            src_ref=a, dst_ref=b, send_sem=send.at[d], recv_sem=recv.at[me],
            device_id=(d // col_n, d % col_n), device_id_type=MESH,
        )

    def left_share(d, act):
        shares(left, 0, lbuf.at[me], d, remote(l_send, l_recv, d), act)

    def right_share(k, d, act):
        shares(right, 1, rbuf.at[k, row * 2 + half], d, remote(r_send, r_recv, d), act)

    def phase(step):
        return ((step + pairs_of_cols - 1) // pairs_of_cols) * (1 + step % (pairs_of_cols - 1))

    def send_left(j, _):
        def one(step, _):
            d = target(phase((step + 1) % pairs_of_cols), j)

            @pl.when(d != me)
            def _():
                left_share(d, begin)

            return 0

        lax.fori_loop(0, pairs_of_cols, one, 0)
        return 0

    def send_right(first, count):
        def one(i, _):
            k = phase(first + i % count)
            d = target(k, i // count)

            @pl.when(d != me)
            def _():
                right_share(k, d, begin)

            return 0

        lax.fori_loop(0, count * slots, one, 0)

    arrival(t_block(row, col), t_recv.at[me])
    for s in range(pairs_of_cols - 1):
        t1_step(s)
        lax.fori_loop(s * slots // pairs_of_cols, (s + 1) * slots // pairs_of_cols, send_left, 0)
    far = pairs_of_cols - 1
    t1_step(far)
    for i in range(pairs_of_cols):
        for e in range(1, row_n):
            t2_copy(i, e).start()
        t3_copy(i, 0).start()
    lax.fori_loop(far * slots // pairs_of_cols, slots, send_left, 0)
    send_right(0, 2)

    for e in range(1, row_n):
        for i in range(pairs_of_cols):
            r, c = (row + e) % row_n, mate(i)
            arrival(t_block(r, c), t_recv.at[r * col_n + c])
            t3_copy(i, e).start()

    for step in range(2, pairs_of_cols):
        send_right(step, 1)

    span = n * a_own
    lane = lax.broadcasted_iota(jnp.int32, (pb, span), 1)
    line = lax.broadcasted_iota(jnp.int32, (pb, span), 0)
    first_at = blocks[0] * n + row * a_own
    second_at = blocks[1] * n
    first = jnp.zeros((pb, span), F32)
    for i in range(a_own):
        first = jnp.where(lane // n == i, eps_v[first_at + i], first)
    den[...] = first

    def add_second(b, _):
        den[...] = jnp.where(lane % n == b, den[...] + eps_v[second_at + b], den[...])
        return 0

    lax.fori_loop(0, n, add_second, 0)
    pair_sum = jnp.zeros((pb, span), F32)
    for i in range(pb):
        at = col * pb + i
        level = eps_o[pairs[0, at]] + eps_o[pairs[1, at]]
        pair_sum = jnp.where(line == i, level, pair_sum)
    den[...] = den[...] - pair_sum

    for e in range(row_n):
        for i in range(pairs_of_cols):
            r, c = (row + e) % row_n, 2 * ((cpair + i) % pairs_of_cols) + 1 - half
            arrival(t_block(r, c), t_recv.at[r * col_n + c])

    def turn_amps(i, _):
        for h in range(2):
            tturn[i, h * width:(h + 1) * width, :] = tbuf[2 * i + h].astype(F32).T.astype(BF16)
        return 0

    if all_p <= width:
        lax.fori_loop(0, all_c // 2, turn_amps, 0)

    def turn_left(a, _):
        share_arrival(lbuf.at[a], l_recv.at[a])
        flipped = lbuf[a].astype(F32).T
        for part in range(kp // 128):
            lturn[part, pl.ds(a, all_c, stride=n), :] = flipped[:, part * 128:(part + 1) * 128]
        return 0

    lax.fori_loop(0, n, turn_left, 0)

    def pack_left(i, _):
        rows = pl.ds(pl.multiple_of(i * 128, 128), 128)
        for part in range(kp // 128):
            lrows[rows, part * 128:(part + 1) * 128] = lturn[part, rows, :].astype(BF16)
        return 0

    lax.fori_loop(0, all_c * n // 128, pack_left, 0)

    cpairs = ybuf.shape[0]
    rows_c = cpairs * 2 * n

    def s1_copy(step, e):
        r, k, slot = (row + e) % row_n, phase(step), step % 2
        return pltpu.make_async_remote_copy(
            src_ref=out1.at[slot, r], dst_ref=in1.at[k, row],
            send_sem=s1_send.at[slot * row_n + r], recv_sem=s1_recv.at[k * row_n + row],
            device_id=(r, col), device_id_type=MESH,
        )

    def chunk(step, _):
        k = phase(step)
        source = 2 * ((cpair + k) % pairs_of_cols)

        def landed(j, _):
            s = (j // 2) * col_n + source + j % 2
            share_arrival(rbuf.at[k, j], r_recv.at[s])
            return 0

        lax.fori_loop(0, slots, landed, 0)
        acc[...] = jnp.zeros_like(acc)

        def some_c(ci, _):
            at = pl.multiple_of(ci * rows_c, rows_c)

            def some_b(j, _):
                weights = jnp.concatenate([rbuf[k, 2 * j], rbuf[k, 2 * j + 1]], axis=1)
                block = jnp.dot(
                    lrows[pl.ds(at, rows_c), :], weights, preferred_element_type=F32
                ).astype(BF16).reshape(cpairs, 2, n, 2 * width)
                for x in range(2):
                    spot = pl.ds(pl.multiple_of((2 * j + x) * n, n), n)
                    for h in range(2):
                        ybuf[:, spot, h * width:(h + 1) * width] = block[
                            :, h, :, x * width:(x + 1) * width
                        ]
                return 0

            lax.fori_loop(0, row_n, some_b, 0)
            total = acc[...]
            for i in range(cpairs):
                at = ci * cpairs + i
                if all_p <= width:
                    total += jnp.dot(ybuf[i], tturn[at], preferred_element_type=F32)
                else:
                    amp = jnp.concatenate([tbuf[2 * at], tbuf[2 * at + 1]], axis=1)
                    total += lax.dot_general(
                        ybuf[i], amp, (((1,), (1,)), ((), ())), preferred_element_type=F32
                    )
            acc[...] = total
            return 0

        lax.fori_loop(0, all_c // (2 * cpairs), some_c, 0)
        @pl.when(step >= 2)
        def _():
            for e in range(1, row_n):
                s1_copy(step, e).wait_send()

        for r in range(row_n):
            out1[step % 2, r] = acc[...].reshape(slots, row_n, a_own, all_p)[:, r]
        for e in range(1, row_n):
            s1_copy(step, e).start()
        in1[k, row] = out1[step % 2, row]
        return 0

    lax.fori_loop(0, pairs_of_cols, chunk, 0)

    def gather_rows(step, _):
        k = phase(step)
        part = in1[k, row]
        for e in range(1, row_n):
            r = (row + e) % row_n
            arrival(in1.at[k, r], s1_recv.at[k * row_n + r])
            part += in1[k, r]
        source = 2 * ((cpair + k) % pairs_of_cols)
        for j in range(slots):
            b = (j // 2) * col_n + source + j % 2
            for x in range(all_p // 128):
                fin[x, pl.ds(b, a_own, stride=n), :] = part[j, :, x * 128:(x + 1) * 128]
        return 0

    lax.fori_loop(0, pairs_of_cols, gather_rows, 0)
    for x in range(all_p // 128):
        out2[x * 128:(x + 1) * 128, :] = fin[x].T

    def s2_copy(e):
        c = (col + e) % col_n
        return pltpu.make_async_remote_copy(
            src_ref=out2.at[pl.ds(c * pb, pb), :], dst_ref=in2.at[col],
            send_sem=s2_send.at[c], recv_sem=s2_recv.at[col],
            device_id=(row, c), device_id_type=MESH,
        )

    for e in range(1, col_n):
        s2_copy(e).start()
    total = out2[pl.ds(pl.multiple_of(col * pb, pb), pb), :]
    for e in range(1, col_n):
        c = (col + e) % col_n
        arrival(in2.at[c], s2_recv.at[c])
        total += in2[c]
    out[...] = (total / den[...]).astype(out.dtype)

    for s in range(pairs_of_cols):
        for up in (False, True):
            @pl.when(t1_when(s, up))
            def _():
                t1_copy(s, up).wait_send()

    for i in range(pairs_of_cols):
        for e in range(row_n):
            if e > 0:
                t2_copy(i, e).wait_send()
            t3_copy(i, e).wait_send()

    for step in range(max(0, pairs_of_cols - 2), pairs_of_cols):
        for e in range(1, row_n):
            s1_copy(step, e).wait_send()

    def drain(e, _):
        d = (me + e) % n
        left_share(d, begun)
        right_share(0, d, begun)
        return 0

    lax.fori_loop(1, n, drain, 0)
    for e in range(1, col_n):
        s2_copy(e).wait_send()


def shards(panel_left, panel_right, amplitudes, eps_virtual, eps_occupied, pair_list, blocks):
    row_n = lax.axis_size("row")
    col_n = lax.axis_size("col")
    n = row_n * col_n
    fit, _, width = panel_left.shape
    pb, cb, _ = amplitudes.shape
    units = -(-fit // 16)
    base, extra = units // n, units % n
    kp = -(-16 * (base + 1) // 128) * 128
    left = panel_left.reshape(fit, width)
    right = panel_right.reshape(fit, width)
    last = 16 * (units - 1)
    tails = jnp.pad(jnp.stack([left[last:], right[last:]]), ((0, 0), (0, 16 * units - fit), (0, 0)))
    amps = jnp.transpose(amplitudes, (1, 0, 2))
    all_c, all_p = cb * row_n, pb * col_n
    halves = col_n // 2
    slots = 2 * row_n
    a_own = n // row_n
    span = n * a_own
    cpairs = max(1, (128 // n) ** 2)
    dma = pltpu.SemaphoreType.DMA
    hbm = pl.BlockSpec(memory_space=pl.ANY)
    smem = pl.BlockSpec(memory_space=pltpu.SMEM)
    flat = pl.pallas_call(
        functools.partial(kernel, row_n, col_n, base, extra),
        out_shape=jax.ShapeDtypeStruct((pb, span), BF16),
        in_specs=[hbm, hbm, hbm, hbm, smem, smem, smem, smem],
        out_specs=pl.BlockSpec(memory_space=pltpu.VMEM),
        scratch_shapes=[
            pltpu.VMEM((n, kp, width), BF16),
            pltpu.VMEM((halves, slots, kp, width), BF16),
            pltpu.VMEM((kp // 128, all_c * n, 128), F32),
            pltpu.VMEM((all_c * n, kp), BF16),
            pltpu.VMEM((all_c, all_p, width), BF16),
            pltpu.VMEM((all_c // 2 if all_p <= width else 1, 2 * width, all_p), BF16),
            pltpu.VMEM((cpairs, slots * n, 2 * width), BF16),
            pltpu.VMEM((slots * n, all_p), F32),
            pltpu.VMEM((2, row_n, slots, a_own, all_p), F32),
            pltpu.VMEM((halves, row_n, slots, a_own, all_p), F32),
            pltpu.VMEM((all_p // 128, span, 128), F32),
            pltpu.VMEM((all_p, span), F32),
            pltpu.VMEM((col_n, pb, span), F32),
            pltpu.VMEM((pb, span), F32),
            dma((n,)), dma((n,)), dma((n,)), dma((n,)),
            dma((2 * halves,)), dma((halves * row_n,)), dma((halves * row_n,)), dma((n,)),
            dma((2 * row_n,)), dma((halves * row_n,)), dma((col_n,)), dma((col_n,)),
        ],
        compiler_params=pltpu.CompilerParams(
            collective_id=0, has_side_effects=True, vmem_limit_bytes=62 * 1024 * 1024
        ),
        cost_estimate=pl.CostEstimate(
            flops=2 * fit * width * width * n, bytes_accessed=4 * fit * width, transcendentals=0
        ),
        name="ladder_exchange",
    )(left, right, tails, amps, eps_virtual, eps_occupied, pair_list.T, blocks)
    return flat.reshape(pb, a_own, n)


def solution(mesh):
    return jax.shard_map(
        shards,
        mesh=mesh,
        in_specs=(
            P(None, ("row", "col"), None),
            P(None, ("row", "col"), None),
            P("col", "row", None),
            P(),
            P(),
            P(),
            P(),
        ),
        out_specs=P("col", "row", None),
        check_vma=False,
    )
```

profile of v0, /device:TPU:0, one launch (start us, length us, event | category | flops | bytes accessed | tf_op | source)
XLA Modules:
  0.0 136.5 jit_solution(4927496339646626586)
XLA Ops:
  0.0 0.7 slice_bitcast_fusion
  0.7 0.6 fusion.2.tails
  1.3 1.6 %copy.10 = bf16[16,32,128]{2,0,1:T(8,128)(2,1)} copy(bf16[16,32,128]{2,1,0:T(8,128)(2,1)} %param.9) | data formatting | bytes 262144 | tf_op args[2]
  2.9 132.2 %ladder_exchange.1 = bf16[16,256]{1,0:T(8,128)(2,1)} custom-call(bf16[5000,128]{1,0:T(8,128)(2,1)} %bitcast.11, bf16[5000,128]{1,0:T(8,128)(2,1)} %bitcast.12, bf16[2,16,128]{2,1,0:T(8,128)(2,1)} %fusion.2.tails, bf16[32,16,128]{2,1,0:T(8,128)(2,1)} %bitcast.10, f32[1600]{0:T(1024)} %eps_v.1, f32[100]{0:T(128)} %eps_o.1, s32[2,128]{1,0:T(2,128)} %bitcast.13, ...), custom_call_target="tpu_custom_call" | custom-call | flops 5242880000 | bytes 2560000 | tf_op jit(solution)/shard_map/ladder_exchange/pallas_call | solution.py:430
  135.1 1.4 %reshape.15 = bf16[16,8,32]{2,1,0:T(8,128)(2,1)} reshape(bf16[16,256]{1,0:T(8,128)(2,1)} %ladder_exchange.1) | data formatting | bytes 16384 | tf_op jit(solution)/shard_map/reshape | solution.py:462
where the time goes:
time: 137 us
  Pallas kernels  132 us (96%)
  local copies, waits for them, and re-layouts  3.71 us (3%)
    pallas_call x1, Pallas kernels, shards(): pl.pallas_call(functools.partial(kernel, row_n, col_n, base, extra), out_...  132 us

commit v1 on v0

--- a/solution.py
+++ b/solution.py
@@ -112,32 +112,12 @@
     def mate(i):
         return 2 * ((cpair + i) % pairs_of_cols) + half
 
-    def t1_copy(s, up):
-        c = 2 * (cpair - s if up else cpair + s) + half
-        to = 2 * (cpair + 1 if up else cpair - 1) + half
+    def t1_copy(i):
         return pltpu.make_async_remote_copy(
-            src_ref=t_block(row, c), dst_ref=t_block(row, c),
-            send_sem=t_send1.at[2 * s + (1 if up else 0)], recv_sem=t_recv.at[row * col_n + c],
-            device_id=(row, to), device_id_type=MESH,
+            src_ref=amps, dst_ref=t_block(row, col),
+            send_sem=t_send1.at[i], recv_sem=t_recv.at[me],
+            device_id=(row, mate(i)), device_id_type=MESH,
         )
-
-    def t1_when(s, up):
-        if up:
-            return (cpair >= s) & (cpair < pairs_of_cols - 1)
-        return (cpair + s < pairs_of_cols) & (cpair > 0)
-
-    def t1_step(s):
-        for up in (False, True):
-            if s > 0:
-                @pl.when(cpair >= s if up else cpair + s < pairs_of_cols)
-                def _():
-                    at = row * col_n + 2 * (cpair - s if up else cpair + s) + half
-                    c = 2 * (cpair - s if up else cpair + s) + half
-                    arrival(t_block(row, c), t_recv.at[at])
-
-            @pl.when(t1_when(s, up))
-            def _():
-                t1_copy(s, up).start()
 
     def t2_copy(i, e):
         c = mate(i)
@@ -200,17 +180,16 @@
 
         lax.fori_loop(0, count * slots, one, 0)
 
-    arrival(t_block(row, col), t_recv.at[me])
-    for s in range(pairs_of_cols - 1):
-        t1_step(s)
-        lax.fori_loop(s * slots // pairs_of_cols, (s + 1) * slots // pairs_of_cols, send_left, 0)
-    far = pairs_of_cols - 1
-    t1_step(far)
+    for i in range(1, pairs_of_cols):
+        t1_copy(i).start()
+    lax.fori_loop(0, slots // 2, send_left, 0)
     for i in range(pairs_of_cols):
+        c = mate(i)
+        arrival(t_block(row, c), t_recv.at[row * col_n + c])
         for e in range(1, row_n):
             t2_copy(i, e).start()
         t3_copy(i, 0).start()
-    lax.fori_loop(far * slots // pairs_of_cols, slots, send_left, 0)
+    lax.fori_loop(slots // 2, slots, send_left, 0)
     send_right(0, 2)
 
     for e in range(1, row_n):
@@ -244,19 +223,6 @@
         pair_sum = jnp.where(line == i, level, pair_sum)
     den[...] = den[...] - pair_sum
 
-    for e in range(row_n):
-        for i in range(pairs_of_cols):
-            r, c = (row + e) % row_n, 2 * ((cpair + i) % pairs_of_cols) + 1 - half
-            arrival(t_block(r, c), t_recv.at[r * col_n + c])
-
-    def turn_amps(i, _):
-        for h in range(2):
-            tturn[i, h * width:(h + 1) * width, :] = tbuf[2 * i + h].astype(F32).T.astype(BF16)
-        return 0
-
-    if all_p <= width:
-        lax.fori_loop(0, all_c // 2, turn_amps, 0)
-
     def turn_left(a, _):
         share_arrival(lbuf.at[a], l_recv.at[a])
         flipped = lbuf[a].astype(F32).T
@@ -274,8 +240,25 @@
 
     lax.fori_loop(0, all_c * n // 128, pack_left, 0)
 
-    cpairs = ybuf.shape[0]
-    rows_c = cpairs * 2 * n
+    c_step = ybuf.shape[2] // width
+    rows_c = c_step * n
+    block_rows = slots * n
+    early = ybuf.shape[0] > 1
+
+    def take_amps():
+        for e in range(row_n):
+            for i in range(pairs_of_cols):
+                r, c = (row + e) % row_n, 2 * ((cpair + i) % pairs_of_cols) + 1 - half
+                arrival(t_block(r, c), t_recv.at[r * col_n + c])
+
+        def turn_amps(i, _):
+            for h in range(4):
+                at = pl.multiple_of((4 * i + h) * width, width)
+                tturn[pl.ds(at, width), :] = tbuf[4 * i + h].astype(F32).T.astype(BF16)
+            return 0
+
+        if early:
+            lax.fori_loop(0, all_c // 4, turn_amps, 0)
 
     def s1_copy(step, e):
         r, k, slot = (row + e) % row_n, phase(step), step % 2
@@ -285,7 +268,7 @@
             device_id=(r, col), device_id_type=MESH,
         )
 
-    def chunk(step, _):
+    def land(step):
         k = phase(step)
         source = 2 * ((cpair + k) % pairs_of_cols)
 
@@ -295,52 +278,97 @@
             return 0
 
         lax.fori_loop(0, slots, landed, 0)
-        acc[...] = jnp.zeros_like(acc)
-
-        def some_c(ci, _):
-            at = pl.multiple_of(ci * rows_c, rows_c)
-
-            def some_b(j, _):
-                weights = jnp.concatenate([rbuf[k, 2 * j], rbuf[k, 2 * j + 1]], axis=1)
-                block = jnp.dot(
-                    lrows[pl.ds(at, rows_c), :], weights, preferred_element_type=F32
-                ).astype(BF16).reshape(cpairs, 2, n, 2 * width)
-                for x in range(2):
-                    spot = pl.ds(pl.multiple_of((2 * j + x) * n, n), n)
-                    for h in range(2):
-                        ybuf[:, spot, h * width:(h + 1) * width] = block[
-                            :, h, :, x * width:(x + 1) * width
-                        ]
-                return 0
-
-            lax.fori_loop(0, row_n, some_b, 0)
-            total = acc[...]
-            for i in range(cpairs):
-                at = ci * cpairs + i
-                if all_p <= width:
-                    total += jnp.dot(ybuf[i], tturn[at], preferred_element_type=F32)
-                else:
-                    amp = jnp.concatenate([tbuf[2 * at], tbuf[2 * at + 1]], axis=1)
-                    total += lax.dot_general(
-                        ybuf[i], amp, (((1,), (1,)), ((), ())), preferred_element_type=F32
-                    )
-            acc[...] = total
-            return 0
-
-        lax.fori_loop(0, all_c // (2 * cpairs), some_c, 0)
+
+    def integrals(step, ci, lead, first_row):
+        k = phase(step)
+        at = pl.multiple_of(ci * rows_c, rows_c)
+
+        def some_b(j, _):
+            weights = jnp.concatenate([rbuf[k, 2 * j], rbuf[k, 2 * j + 1]], axis=1)
+            block = jnp.dot(
+                lrows[pl.ds(at, rows_c), :], weights, preferred_element_type=F32
+            ).astype(BF16).reshape(c_step, n, 2 * width)
+            for x in range(2):
+                spot = pl.ds(pl.multiple_of(first_row + (2 * j + x) * n, n), n)
+                for c in range(c_step):
+                    ybuf[lead, spot, c * width:(c + 1) * width] = block[
+                        c, :, x * width:(x + 1) * width
+                    ]
+            return 0
+
+        lax.fori_loop(0, row_n, some_b, 0)
+
+    def emit(step, first_row):
         @pl.when(step >= 2)
         def _():
             for e in range(1, row_n):
                 s1_copy(step, e).wait_send()
 
+        part = acc[pl.ds(first_row, block_rows), :].reshape(slots, row_n, a_own, all_p)
         for r in range(row_n):
-            out1[step % 2, r] = acc[...].reshape(slots, row_n, a_own, all_p)[:, r]
+            out1[step % 2, r] = part[:, r]
         for e in range(1, row_n):
             s1_copy(step, e).start()
-        in1[k, row] = out1[step % 2, row]
-        return 0
-
-    lax.fori_loop(0, pairs_of_cols, chunk, 0)
+        in1[phase(step), row] = out1[step % 2, row]
+
+    def all_integrals(step, _):
+        land(step)
+        first_row = pl.multiple_of(step * block_rows, block_rows)
+
+        def some_c(ci, _):
+            integrals(step, ci, ci, first_row)
+            return 0
+
+        lax.fori_loop(0, all_c // c_step, some_c, 0)
+        return 0
+
+    def ladder(first_row, rows):
+        acc[pl.ds(0, rows), :] = jnp.zeros((rows, all_p), F32)
+
+        def some_c(ci, _):
+            depth = c_step * width
+            at = pl.multiple_of(ci * depth, depth)
+            acc[pl.ds(0, rows), :] += jnp.dot(
+                ybuf[ci, pl.ds(first_row, rows), :], tturn[pl.ds(at, depth), :],
+                preferred_element_type=F32,
+            )
+            return 0
+
+        lax.fori_loop(0, all_c // c_step, some_c, 0)
+
+    def chunk(step, _):
+        land(step)
+        acc[...] = jnp.zeros_like(acc)
+
+        def some_c(ci, _):
+            integrals(step, ci, 0, 0)
+            amp = jnp.concatenate([tbuf[c_step * ci + c] for c in range(c_step)], axis=1)
+            acc[...] += lax.dot_general(
+                ybuf[0], amp, (((1,), (1,)), ((), ())), preferred_element_type=F32
+            )
+            return 0
+
+        lax.fori_loop(0, all_c // c_step, some_c, 0)
+        emit(step, 0)
+        return 0
+
+    if early:
+        lax.fori_loop(0, 2, all_integrals, 0)
+        take_amps()
+        ladder(0, 2 * block_rows)
+        for step in range(2):
+            emit(step, step * block_rows)
+
+        def later(step, _):
+            all_integrals(step, 0)
+            ladder(pl.multiple_of(step * block_rows, block_rows), block_rows)
+            emit(step, 0)
+            return 0
+
+        lax.fori_loop(2, pairs_of_cols, later, 0)
+    else:
+        take_amps()
+        lax.fori_loop(0, pairs_of_cols, chunk, 0)
 
     def gather_rows(step, _):
         k = phase(step)
@@ -377,12 +405,8 @@
         total += in2[c]
     out[...] = (total / den[...]).astype(out.dtype)
 
-    for s in range(pairs_of_cols):
-        for up in (False, True):
-            @pl.when(t1_when(s, up))
-            def _():
-                t1_copy(s, up).wait_send()
-
+    for i in range(1, pairs_of_cols):
+        t1_copy(i).wait_send()
     for i in range(pairs_of_cols):
         for e in range(row_n):
             if e > 0:
@@ -423,7 +447,8 @@
     slots = 2 * row_n
     a_own = n // row_n
     span = n * a_own
-    cpairs = max(1, (128 // n) ** 2)
+    early = all_c * n * n * width <= 2 ** 24 and all_p <= width
+    c_step = 32 if early else 2
     dma = pltpu.SemaphoreType.DMA
     hbm = pl.BlockSpec(memory_space=pl.ANY)
     smem = pl.BlockSpec(memory_space=pltpu.SMEM)
@@ -438,9 +463,12 @@
             pltpu.VMEM((kp // 128, all_c * n, 128), F32),
             pltpu.VMEM((all_c * n, kp), BF16),
             pltpu.VMEM((all_c, all_p, width), BF16),
-            pltpu.VMEM((all_c // 2 if all_p <= width else 1, 2 * width, all_p), BF16),
-            pltpu.VMEM((cpairs, slots * n, 2 * width), BF16),
-            pltpu.VMEM((slots * n, all_p), F32),
+            pltpu.VMEM((all_c * width if early else 16, all_p), BF16),
+            pltpu.VMEM(
+                (all_c // c_step, n * n, c_step * width) if early else (1, slots * n, c_step * width),
+                BF16,
+            ),
+            pltpu.VMEM((2 * slots * n if early else slots * n, all_p), F32),
             pltpu.VMEM((2, row_n, slots, a_own, all_p), F32),
             pltpu.VMEM((halves, row_n, slots, a_own, all_p), F32),
             pltpu.VMEM((all_p // 128, span, 128), F32),
@@ -448,7 +476,7 @@
             pltpu.VMEM((col_n, pb, span), F32),
             pltpu.VMEM((pb, span), F32),
             dma((n,)), dma((n,)), dma((n,)), dma((n,)),
-            dma((2 * halves,)), dma((halves * row_n,)), dma((halves * row_n,)), dma((n,)),
+            dma((halves,)), dma((halves * row_n,)), dma((halves * row_n,)), dma((n,)),
             dma((2 * row_n,)), dma((halves * row_n,)), dma((col_n,)), dma((col_n,)),
         ],
         compiler_params=pltpu.CompilerParams(

time: 137 us -> 124 us (0.905)
  Pallas kernels: 132 us -> 120 us
    pallas_call x1, Pallas kernels: 132 us -> 120 us  [shards(): pl.pallas_call(functools.partial(kernel, row_n, col_n, base, extra), out_...]
where the time goes in v1:
time: 124 us
  Pallas kernels  120 us (97%)
  local copies, waits for them, and re-layouts  3.71 us (3%)
    pallas_call x1, Pallas kernels, shards(): pl.pallas_call(functools.partial(kernel, row_n, col_n, base, extra), out_...  120 us

profile of v1, /device:TPU:0, one launch (start us, length us, event | category | flops | bytes accessed | tf_op | source)
XLA Modules:
  0.0 124.2 jit_solution(9033309438790089571)
XLA Ops:
  0.0 0.7 slice_bitcast_fusion
  0.7 0.6 fusion.2.tails
  1.3 1.6 %copy.10 = bf16[16,32,128]{2,0,1:T(8,128)(2,1)} copy(bf16[16,32,128]{2,1,0:T(8,128)(2,1)} %param.9) | data formatting | bytes 262144 | tf_op args[2]
  2.9 119.8 %ladder_exchange.1 = bf16[16,256]{1,0:T(8,128)(2,1)} custom-call(bf16[5000,128]{1,0:T(8,128)(2,1)} %bitcast.11, bf16[5000,128]{1,0:T(8,128)(2,1)} %bitcast.12, bf16[2,16,128]{2,1,0:T(8,128)(2,1)} %fusion.2.tails, bf16[32,16,128]{2,1,0:T(8,128)(2,1)} %bitcast.10, f32[1600]{0:T(1024)} %eps_v.1, f32[100]{0:T(128)} %eps_o.1, s32[2,128]{1,0:T(2,128)} %bitcast.13, ...), custom_call_target="tpu_custom_call" | custom-call | flops 5242880000 | bytes 2560000 | tf_op jit(solution)/shard_map/ladder_exchange/pallas_call | solution.py:455
  122.8 1.4 %reshape.15 = bf16[16,8,32]{2,1,0:T(8,128)(2,1)} reshape(bf16[16,256]{1,0:T(8,128)(2,1)} %ladder_exchange.1) | data formatting | bytes 16384 | tf_op jit(solution)/shard_map/reshape | solution.py:490

commit v2 on v1

--- a/solution.py
+++ b/solution.py
@@ -110,13 +110,26 @@
     pl.semaphore_wait(barrier, n - 1)
 
     def mate(i):
-        return 2 * ((cpair + i) % pairs_of_cols) + half
+        other, bit = cpair, 1
+        while bit <= i:
+            if i & bit:
+                other = other + bit * (1 - 2 * ((other // bit) % 2))
+            bit *= 2
+        return 2 * other + half
+
+    hops, bit, held = [], pairs_of_cols // 2, [0]
+    while bit:
+        hops += [(block, bit) for block in held]
+        held += [block + bit for block in held]
+        bit //= 2
 
     def t1_copy(i):
+        block, partner = hops[i]
+        c = mate(block)
         return pltpu.make_async_remote_copy(
-            src_ref=amps, dst_ref=t_block(row, col),
-            send_sem=t_send1.at[i], recv_sem=t_recv.at[me],
-            device_id=(row, mate(i)), device_id_type=MESH,
+            src_ref=t_block(row, c), dst_ref=t_block(row, c),
+            send_sem=t_send1.at[i], recv_sem=t_recv.at[row * col_n + c],
+            device_id=(row, mate(partner)), device_id_type=MESH,
         )
 
     def t2_copy(i, e):
@@ -180,17 +193,29 @@
 
         lax.fori_loop(0, count * slots, one, 0)
 
-    for i in range(1, pairs_of_cols):
-        t1_copy(i).start()
-    lax.fori_loop(0, slots // 2, send_left, 0)
+    here = set()
+
+    def need(block):
+        if block not in here:
+            here.add(block)
+            c = mate(block)
+            arrival(t_block(row, c), t_recv.at[row * col_n + c])
+
+    for own in (True, False):
+        for i, (block, _) in enumerate(hops):
+            if (block == 0) == own:
+                need(block)
+                t1_copy(i).start()
+        lax.fori_loop(0 if own else slots // 4, slots // 4 if own else slots // 2, send_left, 0)
     for i in range(pairs_of_cols):
-        c = mate(i)
-        arrival(t_block(row, c), t_recv.at[row * col_n + c])
+        need(i)
         for e in range(1, row_n):
             t2_copy(i, e).start()
         t3_copy(i, 0).start()
     lax.fori_loop(slots // 2, slots, send_left, 0)
     send_right(0, 2)
+    if pairs_of_cols > 2:
+        send_right(2, 1)
 
     for e in range(1, row_n):
         for i in range(pairs_of_cols):
@@ -198,7 +223,7 @@
             arrival(t_block(r, c), t_recv.at[r * col_n + c])
             t3_copy(i, e).start()
 
-    for step in range(2, pairs_of_cols):
+    for step in range(3, pairs_of_cols):
         send_right(step, 1)
 
     span = n * a_own
@@ -223,14 +248,18 @@
         pair_sum = jnp.where(line == i, level, pair_sum)
     den[...] = den[...] - pair_sum
 
-    def turn_left(a, _):
-        share_arrival(lbuf.at[a], l_recv.at[a])
-        flipped = lbuf[a].astype(F32).T
-        for part in range(kp // 128):
-            lturn[part, pl.ds(a, all_c, stride=n), :] = flipped[:, part * 128:(part + 1) * 128]
-        return 0
-
-    lax.fori_loop(0, n, turn_left, 0)
+    def turn_left(i, _):
+        for x in range(4):
+            share_arrival(lbuf.at[4 * i + x], l_recv.at[4 * i + x])
+        flipped = [lbuf[4 * i + x].astype(F32).T for x in range(4)]
+        for x in range(4):
+            for part in range(kp // 128):
+                lturn[part, pl.ds(4 * i + x, all_c, stride=n), :] = flipped[x][
+                    :, part * 128:(part + 1) * 128
+                ]
+        return 0
+
+    lax.fori_loop(0, n // 4, turn_left, 0)
 
     def pack_left(i, _):
         rows = pl.ds(pl.multiple_of(i * 128, 128), 128)
@@ -405,7 +434,7 @@
         total += in2[c]
     out[...] = (total / den[...]).astype(out.dtype)
 
-    for i in range(1, pairs_of_cols):
+    for i in range(len(hops)):
         t1_copy(i).wait_send()
     for i in range(pairs_of_cols):
         for e in range(row_n):

time: 124 us -> 119 us (0.960)
  Pallas kernels: 120 us -> 114 us
    pallas_call x1, Pallas kernels: 120 us -> 114 us  [shards(): pl.pallas_call(functools.partial(kernel, row_n, col_n, base, extra), out_...]
where the time goes in v2:
time: 119 us; the launch traced here: 118 us
  Pallas kernels  114 us (96%)
  local copies, waits for them, and re-layouts  3.71 us (3%)
    pallas_call x1, Pallas kernels, shards(): pl.pallas_call(functools.partial(kernel, row_n, col_n, base, extra), out_...  114 us

profile of v2, /device:TPU:0, one launch (start us, length us, event | category | flops | bytes accessed | tf_op | source)
XLA Modules:
  0.0 118.4 jit_solution(15671788086843418702)
XLA Ops:
  0.0 0.7 slice_bitcast_fusion
  0.7 0.6 fusion.2.tails
  1.3 1.6 %copy.10 = bf16[16,32,128]{2,0,1:T(8,128)(2,1)} copy(bf16[16,32,128]{2,1,0:T(8,128)(2,1)} %param.9) | data formatting | bytes 262144 | tf_op args[2]
  2.9 114.1 %ladder_exchange.1 = bf16[16,256]{1,0:T(8,128)(2,1)} custom-call(bf16[5000,128]{1,0:T(8,128)(2,1)} %bitcast.11, bf16[5000,128]{1,0:T(8,128)(2,1)} %bitcast.12, bf16[2,16,128]{2,1,0:T(8,128)(2,1)} %fusion.2.tails, bf16[32,16,128]{2,1,0:T(8,128)(2,1)} %bitcast.10, f32[1600]{0:T(1024)} %eps_v.1, f32[100]{0:T(128)} %eps_o.1, s32[2,128]{1,0:T(2,128)} %bitcast.13, ...), custom_call_target="tpu_custom_call" | custom-call | flops 5242880000 | bytes 2560000 | tf_op jit(solution)/shard_map/ladder_exchange/pallas_call | solution.py:484
  117.0 1.4 %reshape.15 = bf16[16,8,32]{2,1,0:T(8,128)(2,1)} reshape(bf16[16,256]{1,0:T(8,128)(2,1)} %ladder_exchange.1) | data formatting | bytes 16384 | tf_op jit(solution)/shard_map/reshape | solution.py:519

commit v3 on v2

--- a/solution.py
+++ b/solution.py
@@ -180,7 +180,7 @@
         lax.fori_loop(0, pairs_of_cols, one, 0)
         return 0
 
-    def send_right(first, count):
+    def send_right(first, count, start, stop):
         def one(i, _):
             k = phase(first + i % count)
             d = target(k, i // count)
@@ -191,7 +191,7 @@
 
             return 0
 
-        lax.fori_loop(0, count * slots, one, 0)
+        lax.fori_loop(count * start, count * stop, one, 0)
 
     here = set()
 
@@ -206,25 +206,15 @@
             if (block == 0) == own:
                 need(block)
                 t1_copy(i).start()
-        lax.fori_loop(0 if own else slots // 4, slots // 4 if own else slots // 2, send_left, 0)
+        lax.fori_loop(0 if own else slots // 4, slots // 4 if own else slots, send_left, 0)
     for i in range(pairs_of_cols):
         need(i)
         for e in range(1, row_n):
             t2_copy(i, e).start()
         t3_copy(i, 0).start()
-    lax.fori_loop(slots // 2, slots, send_left, 0)
-    send_right(0, 2)
-    if pairs_of_cols > 2:
-        send_right(2, 1)
-
-    for e in range(1, row_n):
-        for i in range(pairs_of_cols):
-            r, c = (row + e) % row_n, mate(i)
-            arrival(t_block(r, c), t_recv.at[r * col_n + c])
-            t3_copy(i, e).start()
-
-    for step in range(3, pairs_of_cols):
-        send_right(step, 1)
+        send_right(0, 2, i * slots // pairs_of_cols, (i + 1) * slots // pairs_of_cols)
+    for step in range(2, pairs_of_cols - 1):
+        send_right(step, 1, 0, slots)
 
     span = n * a_own
     lane = lax.broadcasted_iota(jnp.int32, (pb, span), 1)
@@ -248,15 +238,17 @@
         pair_sum = jnp.where(line == i, level, pair_sum)
     den[...] = den[...] - pair_sum
 
+    spans = [(lo, min(lo + 128, most)) for lo in range(0, kp, 128)]
+
     def turn_left(i, _):
         for x in range(4):
             share_arrival(lbuf.at[4 * i + x], l_recv.at[4 * i + x])
-        flipped = [lbuf[4 * i + x].astype(F32).T for x in range(4)]
+        flipped = [
+            [lbuf[4 * i + x, lo:hi, :].astype(F32).T for lo, hi in spans] for x in range(4)
+        ]
         for x in range(4):
-            for part in range(kp // 128):
-                lturn[part, pl.ds(4 * i + x, all_c, stride=n), :] = flipped[x][
-                    :, part * 128:(part + 1) * 128
-                ]
+            for part, (lo, hi) in enumerate(spans):
+                lturn[part, pl.ds(4 * i + x, all_c, stride=n), :hi - lo] = flipped[x][part]
         return 0
 
     lax.fori_loop(0, n // 4, turn_left, 0)
@@ -264,10 +256,23 @@
     def pack_left(i, _):
         rows = pl.ds(pl.multiple_of(i * 128, 128), 128)
         for part in range(kp // 128):
-            lrows[rows, part * 128:(part + 1) * 128] = lturn[part, rows, :].astype(BF16)
+            lo, hi = spans[part]
+            turned = lturn[part, rows, :]
+            if hi - lo < 128:
+                spot = lax.broadcasted_iota(jnp.int32, turned.shape, 1)
+                turned = jnp.where(spot < hi - lo, turned, 0.0)
+            lrows[rows, lo:lo + 128] = turned.astype(BF16)
         return 0
 
     lax.fori_loop(0, all_c * n // 128, pack_left, 0)
+
+    for e in range(1, row_n):
+        for i in range(pairs_of_cols):
+            r, c = (row + e) % row_n, mate(i)
+            arrival(t_block(r, c), t_recv.at[r * col_n + c])
+            t3_copy(i, e).start()
+    if pairs_of_cols > 2:
+        send_right(pairs_of_cols - 1, 1, 0, slots)
 
     c_step = ybuf.shape[2] // width
     rows_c = c_step * n

time: 119 us -> 116 us (0.975)
  Pallas kernels: 114 us -> 111 us
    pallas_call x1, Pallas kernels: 114 us -> 111 us  [shards(): pl.pallas_call(functools.partial(kernel, row_n, col_n, base, extra), out_...]
where the time goes in v3:
time: 116 us; the launch traced here: 115 us
  Pallas kernels  111 us (96%)
  local copies, waits for them, and re-layouts  3.71 us (3%)
    pallas_call x1, Pallas kernels, shards(): pl.pallas_call(functools.partial(kernel, row_n, col_n, base, extra), out_...  111 us

profile of v3, /device:TPU:0, one launch (start us, length us, event | category | flops | bytes accessed | tf_op | source)
XLA Modules:
  0.0 115.4 jit_solution(13431796990820214436)
XLA Ops:
  0.0 0.7 slice_bitcast_fusion
  0.7 0.6 fusion.2.tails
  1.3 1.6 %copy.10 = bf16[16,32,128]{2,0,1:T(8,128)(2,1)} copy(bf16[16,32,128]{2,1,0:T(8,128)(2,1)} %param.9) | data formatting | bytes 262144 | tf_op args[2]
  2.9 111.1 %ladder_exchange.1 = bf16[16,256]{1,0:T(8,128)(2,1)} custom-call(bf16[5000,128]{1,0:T(8,128)(2,1)} %bitcast.11, bf16[5000,128]{1,0:T(8,128)(2,1)} %bitcast.12, bf16[2,16,128]{2,1,0:T(8,128)(2,1)} %fusion.2.tails, bf16[32,16,128]{2,1,0:T(8,128)(2,1)} %bitcast.10, f32[1600]{0:T(1024)} %eps_v.1, f32[100]{0:T(128)} %eps_o.1, s32[2,128]{1,0:T(2,128)} %bitcast.13, ...), custom_call_target="tpu_custom_call" | custom-call | flops 5242880000 | bytes 2560000 | tf_op jit(solution)/shard_map/ladder_exchange/pallas_call | solution.py:489
  114.0 1.4 %reshape.15 = bf16[16,8,32]{2,1,0:T(8,128)(2,1)} reshape(bf16[16,256]{1,0:T(8,128)(2,1)} %ladder_exchange.1) | data formatting | bytes 16384 | tf_op jit(solution)/shard_map/reshape | solution.py:524

commit v4 on v3

--- a/solution.py
+++ b/solution.py
@@ -149,8 +149,8 @@
         )
 
     def target(k, j):
-        spot = (row * 2 + half + j) % slots
-        return (spot // 2) * col_n + 2 * ((cpair + pairs_of_cols - k) % pairs_of_cols) + spot % 2
+        to_row, to_half = (row + j // 2) % row_n, (half + j) % 2
+        return to_row * col_n + 2 * ((cpair + pairs_of_cols - k) % pairs_of_cols) + to_half
 
     def remote(send, recv, d):
         return lambda a, b: pltpu.make_async_remote_copy(
@@ -213,7 +213,7 @@
             t2_copy(i, e).start()
         t3_copy(i, 0).start()
         send_right(0, 2, i * slots // pairs_of_cols, (i + 1) * slots // pairs_of_cols)
-    for step in range(2, pairs_of_cols - 1):
+    for step in range(2, pairs_of_cols):
         send_right(step, 1, 0, slots)
 
     span = n * a_own
@@ -266,13 +266,12 @@
 
     lax.fori_loop(0, all_c * n // 128, pack_left, 0)
 
-    for e in range(1, row_n):
-        for i in range(pairs_of_cols):
-            r, c = (row + e) % row_n, mate(i)
-            arrival(t_block(r, c), t_recv.at[r * col_n + c])
-            t3_copy(i, e).start()
-    if pairs_of_cols > 2:
-        send_right(pairs_of_cols - 1, 1, 0, slots)
+    def share_amps():
+        for e in range(1, row_n):
+            for i in range(pairs_of_cols):
+                r, c = (row + e) % row_n, mate(i)
+                arrival(t_block(r, c), t_recv.at[r * col_n + c])
+                t3_copy(i, e).start()
 
     c_step = ybuf.shape[2] // width
     rows_c = c_step * n
@@ -302,35 +301,25 @@
             device_id=(r, col), device_id_type=MESH,
         )
 
-    def land(step):
+    def land(step, r):
         k = phase(step)
-        source = 2 * ((cpair + k) % pairs_of_cols)
-
-        def landed(j, _):
-            s = (j // 2) * col_n + source + j % 2
-            share_arrival(rbuf.at[k, j], r_recv.at[s])
-            return 0
-
-        lax.fori_loop(0, slots, landed, 0)
-
-    def integrals(step, ci, lead, first_row):
+        source = r * col_n + 2 * ((cpair + k) % pairs_of_cols)
+        for x in range(2):
+            share_arrival(rbuf.at[k, 2 * r + x], r_recv.at[source + x])
+
+    def integrals(step, r, ci, lead, first_row):
         k = phase(step)
         at = pl.multiple_of(ci * rows_c, rows_c)
-
-        def some_b(j, _):
-            weights = jnp.concatenate([rbuf[k, 2 * j], rbuf[k, 2 * j + 1]], axis=1)
-            block = jnp.dot(
-                lrows[pl.ds(at, rows_c), :], weights, preferred_element_type=F32
-            ).astype(BF16).reshape(c_step, n, 2 * width)
-            for x in range(2):
-                spot = pl.ds(pl.multiple_of(first_row + (2 * j + x) * n, n), n)
-                for c in range(c_step):
-                    ybuf[lead, spot, c * width:(c + 1) * width] = block[
-                        c, :, x * width:(x + 1) * width
-                    ]
-            return 0
-
-        lax.fori_loop(0, row_n, some_b, 0)
+        weights = jnp.concatenate([rbuf[k, 2 * r], rbuf[k, 2 * r + 1]], axis=1)
+        block = jnp.dot(
+            lrows[pl.ds(at, rows_c), :], weights, preferred_element_type=F32
+        ).astype(BF16).reshape(c_step, n, 2 * width)
+        for x in range(2):
+            spot = pl.ds(pl.multiple_of(first_row + (2 * r + x) * n, n), n)
+            for c in range(c_step):
+                ybuf[lead, spot, c * width:(c + 1) * width] = block[
+                    c, :, x * width:(x + 1) * width
+                ]
 
     def emit(step, first_row):
         @pl.when(step >= 2)
@@ -346,14 +335,20 @@
         in1[phase(step), row] = out1[step % 2, row]
 
     def all_integrals(step, _):
-        land(step)
         first_row = pl.multiple_of(step * block_rows, block_rows)
 
-        def some_c(ci, _):
-            integrals(step, ci, ci, first_row)
-            return 0
-
-        lax.fori_loop(0, all_c // c_step, some_c, 0)
+        def some_b(j, _):
+            r = (row + row_n - j) % row_n
+            land(step, r)
+
+            def some_c(ci, _):
+                integrals(step, r, ci, ci, first_row)
+                return 0
+
+            lax.fori_loop(0, all_c // c_step, some_c, 0)
+            return 0
+
+        lax.fori_loop(0, row_n, some_b, 0)
         return 0
 
     def ladder(first_row, rows):
@@ -371,11 +366,16 @@
         lax.fori_loop(0, all_c // c_step, some_c, 0)
 
     def chunk(step, _):
-        land(step)
         acc[...] = jnp.zeros_like(acc)
+        for r in range(row_n):
+            land(step, r)
 
         def some_c(ci, _):
-            integrals(step, ci, 0, 0)
+            def some_b(r, _):
+                integrals(step, r, ci, 0, 0)
+                return 0
+
+            lax.fori_loop(0, row_n, some_b, 0)
             amp = jnp.concatenate([tbuf[c_step * ci + c] for c in range(c_step)], axis=1)
             acc[...] += lax.dot_general(
                 ybuf[0], amp, (((1,), (1,)), ((), ())), preferred_element_type=F32
@@ -387,7 +387,9 @@
         return 0
 
     if early:
-        lax.fori_loop(0, 2, all_integrals, 0)
+        all_integrals(0, 0)
+        share_amps()
+        all_integrals(1, 0)
         take_amps()
         ladder(0, 2 * block_rows)
         for step in range(2):
@@ -401,6 +403,7 @@
 
         lax.fori_loop(2, pairs_of_cols, later, 0)
     else:
+        share_amps()
         take_amps()
         lax.fori_loop(0, pairs_of_cols, chunk, 0)
 

time: 116 us -> 115 us (level)
  no operation moved by 1% of the time
where the time goes in v4:
time: 115 us
  Pallas kernels  111 us (97%)
  local copies, waits for them, and re-layouts  3.71 us (3%)
    pallas_call x1, Pallas kernels, shards(): pl.pallas_call(functools.partial(kernel, row_n, col_n, base, extra), out_...  111 us

profile of v4, /device:TPU:0, one launch (start us, length us, event | category | flops | bytes accessed | tf_op | source)
XLA Modules:
  0.0 114.9 jit_solution(7175464353122956288)
XLA Ops:
  0.0 0.7 slice_bitcast_fusion
  0.7 0.6 fusion.2.tails
  1.3 1.6 %copy.10 = bf16[16,32,128]{2,0,1:T(8,128)(2,1)} copy(bf16[16,32,128]{2,1,0:T(8,128)(2,1)} %param.9) | data formatting | bytes 262144 | tf_op args[2]
  2.9 110.6 %ladder_exchange.1 = bf16[16,256]{1,0:T(8,128)(2,1)} custom-call(bf16[5000,128]{1,0:T(8,128)(2,1)} %bitcast.11, bf16[5000,128]{1,0:T(8,128)(2,1)} %bitcast.12, bf16[2,16,128]{2,1,0:T(8,128)(2,1)} %fusion.2.tails, bf16[32,16,128]{2,1,0:T(8,128)(2,1)} %bitcast.10, f32[1600]{0:T(1024)} %eps_v.1, f32[100]{0:T(128)} %eps_o.1, s32[2,128]{1,0:T(2,128)} %bitcast.13, ...), custom_call_target="tpu_custom_call" | custom-call | flops 5242880000 | bytes 2560000 | tf_op jit(solution)/shard_map/ladder_exchange/pallas_call | solution.py:492
  113.5 1.4 %reshape.15 = bf16[16,8,32]{2,1,0:T(8,128)(2,1)} reshape(bf16[16,256]{1,0:T(8,128)(2,1)} %ladder_exchange.1) | data formatting | bytes 16384 | tf_op jit(solution)/shard_map/reshape | solution.py:527

commit v5 on v4

--- a/solution.py
+++ b/solution.py
@@ -206,13 +206,20 @@
             if (block == 0) == own:
                 need(block)
                 t1_copy(i).start()
-        lax.fori_loop(0 if own else slots // 4, slots // 4 if own else slots, send_left, 0)
-    for i in range(pairs_of_cols):
-        need(i)
-        for e in range(1, row_n):
+        if own:
+            lax.fori_loop(0, slots // 4, send_left, 0)
+    waiting = [(i, e) for i in range(pairs_of_cols) for e in range(1, row_n)]
+    lefts = slots - slots // 4
+    groups = lefts + slots // 2
+    for g in range(groups):
+        if g < lefts:
+            send_left(slots // 4 + g, 0)
+        else:
+            send_right(0, 2, 2 * (g - lefts), 2 * (g - lefts) + 2)
+        while len(waiting) * groups > (groups - 1 - g) * pairs_of_cols * (row_n - 1):
+            i, e = waiting.pop(0)
+            need(i)
             t2_copy(i, e).start()
-        t3_copy(i, 0).start()
-        send_right(0, 2, i * slots // pairs_of_cols, (i + 1) * slots // pairs_of_cols)
     for step in range(2, pairs_of_cols):
         send_right(step, 1, 0, slots)
 
@@ -267,10 +274,11 @@
     lax.fori_loop(0, all_c * n // 128, pack_left, 0)
 
     def share_amps():
-        for e in range(1, row_n):
+        for e in range(row_n):
             for i in range(pairs_of_cols):
                 r, c = (row + e) % row_n, mate(i)
-                arrival(t_block(r, c), t_recv.at[r * col_n + c])
+                if e > 0:
+                    arrival(t_block(r, c), t_recv.at[r * col_n + c])
                 t3_copy(i, e).start()
 
     c_step = ybuf.shape[2] // width

time: 115 us -> 115 us (level)
  no operation moved by 1% of the time
where the time goes in v5:
time: 115 us; the launch traced here: 114 us
  Pallas kernels  110 us (96%)
  local copies, waits for them, and re-layouts  3.71 us (3%)
    pallas_call x1, Pallas kernels, shards(): pl.pallas_call(functools.partial(kernel, row_n, col_n, base, extra), out_...  110 us

profile of v5, /device:TPU:0, one launch (start us, length us, event | category | flops | bytes accessed | tf_op | source)
XLA Modules:
  0.0 114.3 jit_solution(8405877139557496313)
XLA Ops:
  0.0 0.7 slice_bitcast_fusion
  0.7 0.6 fusion.2.tails
  1.3 1.6 %copy.10 = bf16[16,32,128]{2,0,1:T(8,128)(2,1)} copy(bf16[16,32,128]{2,1,0:T(8,128)(2,1)} %param.9) | data formatting | bytes 262144 | tf_op args[2]
  2.9 109.9 %ladder_exchange.1 = bf16[16,256]{1,0:T(8,128)(2,1)} custom-call(bf16[5000,128]{1,0:T(8,128)(2,1)} %bitcast.11, bf16[5000,128]{1,0:T(8,128)(2,1)} %bitcast.12, bf16[2,16,128]{2,1,0:T(8,128)(2,1)} %fusion.2.tails, bf16[32,16,128]{2,1,0:T(8,128)(2,1)} %bitcast.10, f32[1600]{0:T(1024)} %eps_v.1, f32[100]{0:T(128)} %eps_o.1, s32[2,128]{1,0:T(2,128)} %bitcast.13, ...), custom_call_target="tpu_custom_call" | custom-call | flops 5242880000 | bytes 2560000 | tf_op jit(solution)/shard_map/ladder_exchange/pallas_call | solution.py:500
  112.9 1.4 %reshape.15 = bf16[16,8,32]{2,1,0:T(8,128)(2,1)} reshape(bf16[16,256]{1,0:T(8,128)(2,1)} %ladder_exchange.1) | data formatting | bytes 16384 | tf_op jit(solution)/shard_map/reshape | solution.py:535
